TPU v7x, 512 devices: a whole 4x4x16 slice. The times are simulated.
512 devices in a mesh: seq: 64 (over z, y_lo, core), tp: 8 (over y_hi, x).
Axes of the slice: x: 4, y: 4 (y_hi: 2, y_lo: 2; y = y_hi * 2 + y_lo), z: 16, core: 2. Of those that a mesh axis runs over, the one named last changes fastest.
Arguments:
- queries: bfloat16 [8192, 1024], P('seq'), may hold values from -8 to 8
- key_rows: bfloat16 [8192, 256], P(('seq', 'tp')), may hold values from -4 to 4
- value_rows: bfloat16 [8192, 256], P(('seq', 'tp')), may hold values from -6 to 6
- ssm_input: bfloat16 [8192, 3072], P('seq', 'tp'), may hold values from -0.29882812 to 0.29882812
- gate_input: bfloat16 [8192, 3072], P('seq', 'tp'), may hold values from -6 to 6
- write_vectors: bfloat16 [8192, 256], P('seq'), may hold values from -1.5 to 1.5
- read_vectors: bfloat16 [8192, 256], P('seq'), may hold values from -1.5 to 1.5
- decay_rates: float32 [8192, 48], P('seq', 'tp'), may hold values from 0 to 3, as said below
- attn_out_weight: bfloat16 [1024, 2048], P('tp'), may hold values from -0.8984375 to 0.8984375
- ssm_out_weight: bfloat16 [3072, 2048], P('tp'), may hold values from -0.109375 to 0.109375
Outputs:
- mixer_output: float32 [8192, 2048], P(('seq', 'tp'))
Inputs may be any that keep to these rules, and one draw needn't show every extreme that they name: `decay_rates`: positive.
All inputs are finite; a program needn't handle non-finite values.
Results may differ from a plain program's by a relative error of at most 0.0045.
Values may be sent and summed in bfloat16 or wider, within the bound.
No kernel may reach another device: no remote copies, remote signals or barrier semaphores. Data moves between devices by JAX's collectives and lax.ppermute only.
A program may use at most 128 MiB of HBM per device.

v0:
```python
import math
import jax
import jax.numpy as jnp
from jax import lax
from jax.sharding import PartitionSpec as P

ASKER_PROBES = 8
KVHEADS = 2
HEAD = 128
precise = lax.Precision.HIGHEST
masked_score = -1e30


def prefix(value, axis, join, neutral):
    count, mine = (lax.axis_size(axis), lax.axis_index(axis))
    pieces = jax.tree.map(lambda part: lax.all_gather(part, axis), value)
    so_far = jax.tree.map(
        lambda part, zero: jnp.full_like(part, 0) + jnp.asarray(zero, part.dtype), value, neutral
    )

    def turn(position, so_far):
        longer = join(so_far, jax.tree.map(lambda part: part[position], pieces))
        return jax.tree.map(lambda new, old: jnp.where(position < mine, new, old), longer, so_far)

    return lax.fori_loop(0, count - 1, turn, so_far)


def combined_all(value, axis, join):
    pieces = jax.tree.map(lambda part: lax.all_gather(part, axis), value)
    head = jax.tree.map(lambda part: part[0], pieces)
    tail = jax.tree.map(lambda part: part[1:], pieces)
    so_far, _ = lax.scan(lambda so_far, slab: (join(so_far, slab), None), head, tail)
    return so_far


def local_states(ssm_input, write_vectors, read_vectors, decay_rates):
    local_rows = ssm_input.shape[0]
    heads_here = decay_rates.shape[1]
    values_f32 = ssm_input.astype(jnp.float32).reshape(local_rows, heads_here, -1)
    write_f32 = write_vectors.astype(jnp.float32)
    read_f32 = read_vectors.astype(jnp.float32)
    decay_sum = jnp.cumsum(-decay_rates, axis=0)
    block_decay = decay_sum[-1]
    positions = jnp.arange(local_rows)
    causal = (positions[:, None] >= positions[None, :])[:, :, None]
    decay_gap = jnp.where(causal, decay_sum[:, None, :] - decay_sum[None, :, :], 0.0)
    read_write = jnp.dot(read_vectors, write_vectors.T, preferred_element_type=jnp.float32)
    factor = jnp.where(causal, jnp.exp(decay_gap), 0.0) * read_write[:, :, None]
    within = jnp.einsum("tsh,shp->thp", factor, values_f32, precision=precise)
    block_state = jnp.einsum(
        "sh,shp,sn->hpn",
        jnp.exp(block_decay[None, :] - decay_sum),
        values_f32,
        write_f32,
        precision=precise,
    )
    return (within, block_state, decay_sum, read_f32)


def combine_states(earlier, later):
    return (earlier[0] * later[0], later[0][:, None, None] * earlier[1] + later[1])


def join_partial(first_part, second_part):
    updated_peak = jnp.maximum(first_part[0], second_part[0])
    first_scale = jnp.exp(first_part[0] - updated_peak)
    second_scale = jnp.exp(second_part[0] - updated_peak)
    running_sum = first_part[1] * first_scale + second_part[1] * second_scale
    weighted = first_part[2] * first_scale[..., None] + second_part[2] * second_scale[..., None]
    return (updated_peak, running_sum, weighted)


def local(
    queries,
    key_rows,
    value_rows,
    ssm_input,
    gate_input,
    write_vectors,
    read_vectors,
    decay_rates,
    attn_out_weight,
    ssm_out_weight,
):
    local_rows = queries.shape[0]
    within, block_state, decay_sum, read_f32 = local_states(
        ssm_input, write_vectors, read_vectors, decay_rates
    )
    block_decay = jnp.exp(decay_sum[-1])
    neutral = (jnp.ones_like(block_decay), jnp.zeros_like(block_state))
    entering = prefix((block_decay, block_state), "seq", combine_states, neutral)
    carried = jnp.einsum(
        "th,tn,hpn->thp", jnp.exp(decay_sum), read_f32, entering[1], precision=precise
    )
    ssm_raw = (within + carried).reshape(local_rows, -1)
    ssm_half = (ssm_raw * jax.nn.silu(gate_input.astype(jnp.float32))).astype(jnp.bfloat16)
    group = ASKER_PROBES // KVHEADS
    query_heads = queries.reshape(local_rows, KVHEADS, group, HEAD)
    slice_rows = key_rows.shape[0]
    seq_index = lax.axis_index("seq")
    tp_index = lax.axis_index("tp")
    query_place = seq_index * local_rows + jnp.arange(local_rows)
    score_scale = 1.0 / math.sqrt(HEAD)
    start_max = jnp.full((local_rows, KVHEADS, group), masked_score, jnp.float32)
    start_sum = jnp.zeros((local_rows, KVHEADS, group), jnp.float32)
    start_weighted = jnp.zeros((local_rows, KVHEADS, group, HEAD), jnp.float32)
    running = (start_max, start_sum, start_weighted)
    first_row = jnp.int32(0)
    key_segment = lax.all_gather(key_rows, "seq", axis=0, tiled=True)
    value_part = lax.all_gather(value_rows, "seq", axis=0, tiled=True)
    piece_rows = key_segment.shape[0]
    for lower_row in range(0, piece_rows, 256):
        upper_row = min(lower_row + 256, piece_rows)
        attend_key_segment = key_segment[lower_row:upper_row]
        attend_value_part = value_part[lower_row:upper_row]
        attend_first_row = first_row + lower_row
        attend_piece_rows = attend_key_segment.shape[0]
        row_ids = attend_first_row + jnp.arange(attend_piece_rows)
        key_place = (
            row_ids // slice_rows * local_rows + tp_index * slice_rows + row_ids % slice_rows
        )
        compute_running_max, compute_running_sum, compute_weighted = running
        key_block = attend_key_segment.reshape(attend_piece_rows, KVHEADS, HEAD)
        value_block = attend_value_part.reshape(attend_piece_rows, KVHEADS, HEAD)
        scores = (
            jnp.einsum("tgqd,ngd->tgqn", query_heads, key_block, preferred_element_type=jnp.float32)
            * score_scale
        )
        visible = (key_place[None, :] <= query_place[:, None])[:, None, None, :]
        scores = jnp.where(visible, scores, masked_score)
        updated_peak = jnp.maximum(compute_running_max, jnp.max(scores, axis=-1))
        weights = jnp.where(visible, jnp.exp(scores - updated_peak[..., None]), 0.0)
        factor = jnp.exp(compute_running_max - updated_peak)
        compute_running_sum = compute_running_sum * factor + jnp.sum(weights, axis=-1)
        compute_weighted = compute_weighted * factor[..., None] + jnp.einsum(
            "tgqn,ngd->tgqd",
            weights.astype(jnp.bfloat16),
            value_block,
            preferred_element_type=jnp.float32,
        )
        running = (updated_peak, compute_running_sum, compute_weighted)
    running_max, running_sum, weighted = running
    heads_mine = ASKER_PROBES // lax.axis_size("tp")
    running_max, running_sum, weighted = combined_all(
        (running_max, running_sum, weighted), "tp", join_partial
    )
    all_heads = (weighted / running_sum[..., None]).reshape(local_rows, ASKER_PROBES, HEAD)
    own_heads = lax.dynamic_slice_in_dim(all_heads, tp_index * heads_mine, heads_mine, 1)
    attn_half = own_heads.reshape(local_rows, heads_mine * HEAD).astype(jnp.bfloat16)
    attention_share = lax.psum_scatter(
        jnp.dot(attn_half, attn_out_weight, preferred_element_type=jnp.float32),
        "tp",
        scatter_dimension=0,
        tiled=True,
    )
    state_share = lax.psum_scatter(
        jnp.dot(ssm_half, ssm_out_weight, preferred_element_type=jnp.float32),
        "tp",
        scatter_dimension=0,
        tiled=True,
    )
    summed = attention_share + state_share
    return summed


def solution(mesh):
    placed = (
        P("seq", None),
        P(("seq", "tp"), None),
        P(("seq", "tp"), None),
        P("seq", "tp"),
        P("seq", "tp"),
        P("seq", None),
        P("seq", None),
        P("seq", "tp"),
        P("tp", None),
        P("tp", None),
    )
    return jax.shard_map(
        local, mesh=mesh, in_specs=placed, out_specs=P(("seq", "tp"), None), check_vma=False
    )
```

profile of v0, /device:TPU:2, one launch (start us, length us, event | category | flops | bytes accessed | tf_op | source)
XLA Modules:
  0.0 597.1 jit_solution(9801647952218511953)
XLA Ops:
  6.6 1.2 reshape.438
  7.8 71.4 %all_gather.30 = bf16[1024,256]{1,0:T(8,128)(2,1)S(1)} all-gather(bf16[16,256]{1,0:T(8,128)(2,1)} %param.15), channel_id=1, replica_groups=mesh['seq'=64,'tp'=8] {'seq'}, dimensions={0}, use_global_device_ids=true | all-gather | bytes 532480 | tf_op jit(solution)/shard_map/all_gather | solution.py:109
  80.3 61.2 %all_gather.33 = bf16[1024,256]{1,0:T(8,128)(2,1)S(1)} all-gather(bf16[16,256]{1,0:T(8,128)(2,1)} %param.16), channel_id=1, replica_groups=mesh['seq'=64,'tp'=8] {'seq'}, dimensions={0}, use_global_device_ids=true | all-gather | bytes 532480 | tf_op jit(solution)/shard_map/all_gather | solution.py:110
  144.2 1.3 fusion.106
  148.0 1.7 fusion.19
  152.8 1.4 fusion.23
  154.2 1.4 fusion.25
  155.6 1.4 fusion.27
  158.0 34.1 %all_gather.32 = f32[8,128,2,4]{1,3,2,0:T(4,128)S(1)} all-gather(f32[1,128,2,4]{1,3,2,0:T(4,128)S(1)} %get-tuple-element.225), channel_id=1, replica_groups=mesh['seq'=64,'tp'=8] {'tp'}, dimensions={0}, use_global_device_ids=true | all-gather | bytes 36864 | tf_op jit(solution)/shard_map/all_gather | solution.py:29
  192.0 34.1 %all_gather.31 = f32[8,128,2,4]{1,3,2,0:T(4,128)S(1)} all-gather(f32[1,128,2,4]{1,3,2,0:T(4,128)S(1)} %get-tuple-element.226), channel_id=1, replica_groups=mesh['seq'=64,'tp'=8] {'tp'}, dimensions={0}, use_global_device_ids=true | all-gather | bytes 36864 | tf_op jit(solution)/shard_map/all_gather | solution.py:29
  226.2 62.5 %all-gather.2 = f32[64,1,6]{2,1,0:T(1,128)} all-gather(f32[1,1,6]{2,1,0:T(1,128)S(1)} %copy-done.21), channel_id=1, replica_groups=mesh['seq'=64,'tp'=8] {'seq'}, dimensions={0}, use_global_device_ids=true | all-gather | bytes 1560 | tf_op jit(solution)/shard_map/all_gather | solution.py:16
  288.9 1.3 convolution_bitcast_fusion.5
  291.7 4.2 slice.76
  295.8 18.7 %while.28 = (s32[]{:T(128)}, f32[128,2,4]{0,2,1:T(4,128)S(1)}, f32[128,2,4]{0,2,1:T(4,128)S(1)}, f32[128,2,4,128]{3,2,1,0:T(4,128)S(1)}, f32[7,128,2,4]{1,3,2,0:...) while((s32[]{:T(128)}, f32[128,2,4]{0,2,1:T(4,128)S(1)}, ...), condition=%wide.region_9.10_spmd, body=%wide.region_8.9_spmd.sunk | while | flops 399362 | bytes 2678885 | solution.py:32
  297.3 1.2 fusion.126
  299.9 1.2 fusion.126
  301.5 1.1 constant_dynamic-slice_fusion.2
  302.6 1.2 fusion.126
  305.3 1.2 fusion.126
  306.8 1.1 constant_dynamic-slice_fusion.2
  308.0 1.2 fusion.126
  310.6 1.2 fusion.126
  312.2 1.1 constant_dynamic-slice_fusion.2
  313.3 1.2 fusion.126
  315.4 72.6 %all-gather.8.cloned.1.call-done = f32[384,64,256]{2,1,0:T(8,128)} async-done(((f32[6,64,256]{2,1,0:T(8,128)}), f32[384,64,256]{2,1,0:T(8,128)}) %all-gather.8.cloned.1.call-update) | async-done | bytes 25165840 | tf_op jit(solution)/shard_map/all_gather | solution.py:16
  388.0 114.7 %while.29 = (s32[]{:T(128)}, f32[6,64,256]{2,1,0:T(8,128)S(1)}, s32[]{:T(128)}, f32[64,6]{1,0:T(8,128)}, f32[64,6,64,256]{3,2,1,0:T(8,128)}, /*index=5*/s32[]{:T(128)}, s32[]{:T(128)}) while((s32[]{:T(128)}, f32[6,64,256]{2,1,0:T(8,128)S(1)}, s32[]{:T(128)}, f32[64,6]{1,0:T(8,128)}, f32[64,6,64,256]{3,2,1,0:T(8,128)}, ...), condition=%wide.region_13.14_spmd.clone, body=%wide.region_12.13_spmd.clone.sunk | while | flops 393220 | bytes 1179833 | solution.py:25
  388.7 1.1 fusion.127
  390.5 1.1 fusion.127
  392.3 1.1 fusion.127
  394.2 1.1 fusion.127
  396.0 1.1 fusion.127
  397.8 1.1 fusion.127
  399.6 1.1 fusion.127
  401.5 1.1 fusion.127
  403.3 1.1 fusion.127
  405.1 1.1 fusion.127
  406.9 1.1 fusion.127
  408.8 1.1 fusion.127
  410.6 1.1 fusion.127
  412.4 1.1 fusion.127
  414.2 1.1 fusion.127
  416.1 1.1 fusion.127
  417.9 1.1 fusion.127
  419.7 1.1 fusion.127
  421.5 1.1 fusion.127
  490.7 1.1 fusion.127
  503.2 2.3 convolution_add_fusion
  505.6 85.0 %reduce-scatter.2.cloned.1.call-done = f32[16,2048]{1,0:T(8,128)} async-done(((f32[128,2048]{1,0:T(8,128)}), f32[16,2048]{1,0:T(8,128)}) %reduce-scatter.2.cloned.1.call-update) | async-done | bytes 131088 | tf_op jit(solution)/shard_map/reduce_scatter | solution.py:150
  (232 shorter events, 110.5 us)
Async XLA Ops:
  6.5 496.7 %copy-start = (bf16[384,2048]{1,0:T(8,128)(2,1)S(1)}, bf16[384,2048]{1,0:T(8,128)(2,1)}, u32[]{:S(2)}) copy-start(bf16[384,2048]{1,0:T(8,128)(2,1)} %param.23) | copy-start | bytes 4718596
  6.5 283.7 %all-gather.6.cloned.1.call-start = ((), (), s32[]{:S(2)}) async-start(), calls=%async_computation.1 | async-start | bytes 4718592 | tf_op jit(solution)/shard_map/all_gather | solution.py:29
  143.9 2.8 copy-start.7
  144.2 3.0 copy-start.6
  145.5 2.1 copy-start.13
  145.5 2.1 copy-start.5
  145.9 1.2 copy-start.14
  145.9 2.1 copy-start.1
  146.3 1.7 copy-start.2
  146.3 1.7 copy-start.15
  146.7 1.3 copy-start.3
  146.7 1.3 copy-start.17
  147.1 2.6 copy-start.20
  147.1 3.5 copy-start.12
  147.1 3.7 copy-start.8
  149.7 139.0 %copy-start.9 = (bf16[128,256]{1,0:T(8,128)(2,1)S(1)}, bf16[128,256]{1,0:T(8,128)(2,1)}, u32[]{:S(2)}) copy-start(bf16[128,256]{1,0:T(8,128)(2,1)} %param.20) | copy-start | bytes 196612
  149.7 238.3 %all-gather.8.cloned.1.call-start = ((), (), s32[]{:S(2)}) async-start(), calls=%async_computation.2 | async-start | bytes 25559040 | tf_op jit(solution)/shard_map/all_gather | solution.py:16
  150.8 6.4 %copy-start.16 = (f32[128,2,4]{0,2,1:T(4,128)S(1)}, f32[128,2,4]{0,2,1:T(4,128)}, u32[]{:S(2)}) copy-start(f32[128,2,4]{0,2,1:T(4,128)} %copy-done.15) | copy-start | bytes 12292
  150.8 6.4 %copy-start.18 = (f32[128,2,4]{0,2,1:T(4,128)S(1)}, f32[128,2,4]{0,2,1:T(4,128)}, u32[]{:S(2)}) copy-start(f32[128,2,4]{0,2,1:T(4,128)} %copy-done.17) | copy-start | bytes 12292
  150.9 75.3 %copy-start.21 = (f32[1,1,6]{2,1,0:T(1,128)S(1)}, f32[1,1,6]{2,1,0:T(1,128)}, u32[]{:S(2)}) copy-start(f32[1,1,6]{2,1,0:T(1,128)} %get-tuple-element.224) | copy-start | bytes 76
  152.0 438.6 %reduce-scatter.2.cloned.1.call-start = ((), (), s32[]{:S(2)}) async-start(), calls=%async_computation.3 | async-start | bytes 1179648 | tf_op jit(solution)/shard_map/reduce_scatter | solution.py:150
  295.8 19.2 %copy-start.4 = (bf16[128,2048]{1,0:T(8,128)(2,1)S(1)}, bf16[128,2048]{1,0:T(8,128)(2,1)}, u32[]{:S(2)}) copy-start(bf16[128,2048]{1,0:T(8,128)(2,1)} %param.22) | copy-start | bytes 1572868
  315.1 187.6 %copy-start.19 = (f32[128,6]{0,1:T(8,128)S(1)}, f32[128,6]{0,1:T(8,128)}, u32[]{:S(2)}) copy-start(f32[128,6]{0,1:T(8,128)} %copy.97) | copy-start | bytes 9220
  315.4 187.4 %copy-start.10 = (bf16[128,256]{1,0:T(8,128)(2,1)S(1)}, bf16[128,256]{1,0:T(8,128)(2,1)}, u32[]{:S(2)}) copy-start(bf16[128,256]{1,0:T(8,128)(2,1)} %param.20) | copy-start | bytes 196612
  315.4 187.4 %copy-start.11 = (f32[128,6,64]{0,2,1:T(8,128)S(1)}, f32[128,6,64]{0,2,1:T(8,128)}, u32[]{:S(2)}) copy-start(f32[128,6,64]{0,2,1:T(8,128)} %convolution_bitcast_fusion.5) | copy-start | bytes 589828
Sparse Core Ops, SparseCore 0:
  149.8 81.3 all-gather.5
  233.4 154.5 all-gather.7
  505.7 84.7 reduce-scatter.1
where the time goes:
time: 602 us; the launch traced here: 597 us
  blocking collectives  263 us (44%)
  waiting for transfers between devices  158 us (26%)
  other arithmetic  84.3 us (14%)
  local copies, waits for them, and re-layouts  65.5 us (11%)
  between operations  13.6 us (2%)
  matrix products  10.7 us (2%)
    reduce_scatter x1, waiting for transfers between devices, local(): lax.psum_scatter(jnp.dot(attn_half, attn_out_weight, preferred_element_ty...  85 us
    all_gather x1, waiting for transfers between devices, prefix(): pieces = jax.tree.map(lambda part: lax.all_gather(part, axis), value)  72.6 us
    all_gather x1, blocking collectives, local(): key_segment = lax.all_gather(key_rows, 'seq', axis=0, tiled=True)  71.4 us
    select_n x63, other arithmetic, turn(): jnp.where(position < mine, new, old)  69.8 us
    all_gather x2, blocking collectives, combined_all(): pieces = jax.tree.map(lambda part: lax.all_gather(part, axis), value)  68.2 us
    all_gather x1, blocking collectives, prefix(): pieces = jax.tree.map(lambda part: lax.all_gather(part, axis), value)  62.5 us
    all_gather x1, blocking collectives, local(): value_part = lax.all_gather(value_rows, 'seq', axis=0, tiled=True)  61.2 us
    mul x63, local copies, waits for them, and re-layouts, combine_states(): later[0][:, None, None] * earlier[1] + later[1]  43.3 us
  transfers between devices with their start and end apart: 3, of which 2 were waited for; matrix products, arithmetic and copies ran while one was open for 6% of the time, Pallas kernels for 0%

commit v1 on v0

--- a/solution.py
+++ b/solution.py
@@ -9,6 +9,11 @@
 HEAD = 128
 precise = lax.Precision.HIGHEST
 masked_score = -1e30
+
+
+def gather_over(x, axis, along):
+    outgoing = jnp.stack([x] * lax.axis_size(axis))
+    return jnp.concatenate(lax.all_to_all(outgoing, axis, 0, 0), axis=along)
 
 
 def prefix(value, axis, join, neutral):
@@ -107,7 +112,7 @@
     running = (start_max, start_sum, start_weighted)
     first_row = jnp.int32(0)
     key_segment = lax.all_gather(key_rows, "seq", axis=0, tiled=True)
-    value_part = lax.all_gather(value_rows, "seq", axis=0, tiled=True)
+    value_part = gather_over(value_rows, "seq", 0)
     piece_rows = key_segment.shape[0]
     for lower_row in range(0, piece_rows, 256):
         upper_row = min(lower_row + 256, piece_rows)

time: 602 us -> 588 us (0.977)
  blocking collectives: 263 us -> 211 us
  starting transfers between devices: 0.09 us -> 17.2 us
  matrix products: 10.7 us -> 17.6 us
    all_gather x1 -> x0, blocking collectives: 61.2 us -> none  [local(): value_part = lax.all_gather(value_rows, 'seq', axis=0, tiled=True)]
    all_to_all x0 -> x1, starting transfers between devices: none -> 17.1 us  [gather_over(): return jnp.concatenate(lax.all_to_all(outgoing, axis, 0, 0), axis=along)]
    all_gather x1, blocking collectives: 71.4 us -> 80.1 us  [local(): key_segment = lax.all_gather(key_rows, 'seq', axis=0, tiled=True)]
  transfers between devices with their start and end apart: 3 -> 4, of which waited for: 2 -> 2; matrix products, arithmetic and copies ran while one was open for 6% -> 9% of each run, Pallas kernels for 0% -> 0%
where the time goes in v1:
time: 588 us; the launch traced here: 582 us
  blocking collectives  211 us (36%)
  waiting for transfers between devices  160 us (27%)
  other arithmetic  89.2 us (15%)
  local copies, waits for them, and re-layouts  71.2 us (12%)
  matrix products  17.6 us (3%)
  starting transfers between devices  17.2 us (3%)
  between operations  13.5 us (2%)
    reduce_scatter x1, waiting for transfers between devices, local(): lax.psum_scatter(jnp.dot(attn_half, attn_out_weight, preferred_element_ty...  84.8 us
    all_gather x1, blocking collectives, local(): key_segment = lax.all_gather(key_rows, 'seq', axis=0, tiled=True)  80.1 us
    all_gather x1, waiting for transfers between devices, prefix(): pieces = jax.tree.map(lambda part: lax.all_gather(part, axis), value)  75.5 us
    select_n x63, other arithmetic, turn(): jnp.where(position < mine, new, old)  69.8 us
    all_gather x2, blocking collectives, combined_all(): pieces = jax.tree.map(lambda part: lax.all_gather(part, axis), value)  68.2 us
    all_gather x1, blocking collectives, prefix(): pieces = jax.tree.map(lambda part: lax.all_gather(part, axis), value)  62.9 us
    mul x63, local copies, waits for them, and re-layouts, combine_states(): later[0][:, None, None] * earlier[1] + later[1]  43.1 us
    all_to_all x1, starting transfers between devices, gather_over(): return jnp.concatenate(lax.all_to_all(outgoing, axis, 0, 0), axis=along)  17.1 us
  transfers between devices with their start and end apart: 4, of which 2 were waited for; matrix products, arithmetic and copies ran while one was open for 9% of the time, Pallas kernels for 0%

profile of v1, /device:TPU:2, one launch (start us, length us, event | category | flops | bytes accessed | tf_op | source)
XLA Modules:
  0.0 582.2 jit_solution(8685245784564562498)
XLA Ops:
  6.5 1.7 stack.2
  8.2 17.1 %all-to-all-start = ((bf16[64,16,256]{2,1,0:T(8,128)(2,1)}), bf16[64,16,256]{2,1,0:T(8,128)(2,1)S(1)}, u32[]{:S(2)}, u32[]{:S(2)}) async-start(bf16[64,16,256]{2,1,0:T(8,128)(2,1)} %stack.2), calls=%async_computation | async-start | bytes 1048576 | tf_op jit(solution)/shard_map/all_to_all | solution.py:16
  25.4 80.1 %all_gather.27 = bf16[1024,256]{1,0:T(8,128)(2,1)S(1)} all-gather(bf16[16,256]{1,0:T(8,128)(2,1)} %param.15), channel_id=1, replica_groups=mesh['seq'=64,'tp'=8] {'seq'}, dimensions={0}, use_global_device_ids=true | all-gather | bytes 532480 | tf_op jit(solution)/shard_map/all_gather | solution.py:114
  105.5 1.1 reshape.449
  109.9 1.3 fusion.108
  111.2 2.3 fusion.107
  114.1 2.2 fusion.109
  116.9 1.3 fusion.110
  123.5 1.8 convolution_bitcast_fusion.1
  125.8 2.4 fusion.19
  130.7 1.5 fusion.23
  132.4 1.4 fusion.27
  134.1 34.1 %all_gather.29 = f32[8,128,2,4]{1,3,2,0:T(4,128)S(1)} all-gather(f32[1,128,2,4]{1,3,2,0:T(4,128)S(1)} %get-tuple-element.225), channel_id=1, replica_groups=mesh['seq'=64,'tp'=8] {'tp'}, dimensions={0}, use_global_device_ids=true | all-gather | bytes 36864 | tf_op jit(solution)/shard_map/all_gather | solution.py:34
  168.8 34.1 %all_gather.28 = f32[8,128,2,4]{1,3,2,0:T(4,128)S(1)} all-gather(f32[1,128,2,4]{1,3,2,0:T(4,128)S(1)} %get-tuple-element.226), channel_id=1, replica_groups=mesh['seq'=64,'tp'=8] {'tp'}, dimensions={0}, use_global_device_ids=true | all-gather | bytes 36864 | tf_op jit(solution)/shard_map/all_gather | solution.py:34
  203.5 62.9 %all-gather.2 = f32[64,1,6]{2,1,0:T(1,128)} all-gather(f32[1,1,6]{2,1,0:T(1,128)S(1)} %get-tuple-element.224), channel_id=1, replica_groups=mesh['seq'=64,'tp'=8] {'seq'}, dimensions={0}, use_global_device_ids=true | all-gather | bytes 1560 | tf_op jit(solution)/shard_map/all_gather | solution.py:21
  266.6 1.3 convolution_bitcast_fusion.5
  267.9 1.1 slice.77
  269.4 4.1 slice.80
  273.5 23.5 %while.28 = (s32[]{:T(128)}, f32[128,2,4]{0,2,1:T(4,128)S(1)}, f32[128,2,4]{0,2,1:T(4,128)S(1)}, f32[128,2,4,128]{3,2,1,0:T(4,128)S(1)}, f32[7,128,2,4]{1,3,2,0:...) while((s32[]{:T(128)}, f32[128,2,4]{0,2,1:T(4,128)S(1)}, ...), condition=%wide.region_9.10_spmd, body=%wide.region_8.9_spmd.sunk | while | flops 399362 | bytes 2678885 | solution.py:37
  275.7 1.2 fusion.126
  279.1 1.2 fusion.126
  282.4 1.2 fusion.126
  285.8 1.2 fusion.126
  289.1 1.2 fusion.126
  292.5 1.2 fusion.126
  295.8 1.2 fusion.126
  297.9 75.5 %all-gather.8.cloned.1.call-done = f32[384,64,256]{2,1,0:T(8,128)} async-done(((f32[6,64,256]{2,1,0:T(8,128)}), f32[384,64,256]{2,1,0:T(8,128)}) %all-gather.8.cloned.1.call-update) | async-done | bytes 25165840 | tf_op jit(solution)/shard_map/all_gather | solution.py:21
  373.4 114.6 %while.29 = (s32[]{:T(128)}, f32[6,64,256]{2,1,0:T(8,128)S(1)}, s32[]{:T(128)}, f32[64,6]{1,0:T(8,128)}, f32[64,6,64,256]{3,2,1,0:T(8,128)}, /*index=5*/s32[]{:T(128)}, s32[]{:T(128)}) while((s32[]{:T(128)}, f32[6,64,256]{2,1,0:T(8,128)S(1)}, s32[]{:T(128)}, f32[64,6]{1,0:T(8,128)}, f32[64,6,64,256]{3,2,1,0:T(8,128)}, ...), condition=%wide.region_13.14_spmd.clone, body=%wide.region_12.13_spmd.clone.sunk | while | flops 393220 | bytes 1179833 | solution.py:30
  374.1 1.1 fusion.127
  375.9 1.1 fusion.127
  377.7 1.1 fusion.127
  379.5 1.1 fusion.127
  381.3 1.1 fusion.127
  383.2 1.1 fusion.127
  385.0 1.1 fusion.127
  386.8 1.1 fusion.127
  388.6 1.1 fusion.127
  390.4 1.1 fusion.127
  392.3 1.1 fusion.127
  394.1 1.1 fusion.127
  395.9 1.1 fusion.127
  397.7 1.1 fusion.127
  399.5 1.1 fusion.127
  401.4 1.1 fusion.127
  461.3 1.1 fusion.127
  475.9 1.1 fusion.127
  488.5 2.4 convolution_add_fusion
  490.8 84.8 %reduce-scatter.2.cloned.1.call-done = f32[16,2048]{1,0:T(8,128)} async-done(((f32[128,2048]{1,0:T(8,128)}), f32[16,2048]{1,0:T(8,128)}) %reduce-scatter.2.cloned.1.call-update) | async-done | bytes 131088 | tf_op jit(solution)/shard_map/reduce_scatter | solution.py:155
  (234 shorter events, 124.0 us)
Async XLA Ops:
  6.5 481.9 %copy-start = (bf16[384,2048]{1,0:T(8,128)(2,1)S(1)}, bf16[384,2048]{1,0:T(8,128)(2,1)}, u32[]{:S(2)}) copy-start(bf16[384,2048]{1,0:T(8,128)(2,1)} %param.23) | copy-start | bytes 4718596
  8.2 111.2 %all-to-all-start = ((bf16[64,16,256]{2,1,0:T(8,128)(2,1)}), bf16[64,16,256]{2,1,0:T(8,128)(2,1)S(1)}, u32[]{:S(2)}, u32[]{:S(2)}) async-start(bf16[64,16,256]{2,1,0:T(8,128)(2,1)} %stack.2), calls=%async_computation | async-start | bytes 1048576 | tf_op jit(solution)/shard_map/all_to_all | solution.py:16
  25.3 242.6 %all-gather.6.cloned.1.call-start = ((), (), s32[]{:S(2)}) async-start(), calls=%async_computation.2 | async-start | bytes 4718592 | tf_op jit(solution)/shard_map/all_gather | solution.py:34
  109.7 7.3 %copy-start.4 = (bf16[256,256]{0,1:T(8,128)(2,1)S(1)}, bf16[256,256]{0,1:T(8,128)(2,1)}, u32[]{:S(2)}) copy-start(bf16[256,256]{0,1:T(8,128)(2,1)} %copy.127) | copy-start | bytes 393220
  111.1 5.2 copy-start.11
  113.4 4.8 copy-start.13
  116.3 2.0 copy-start.15
  118.2 0.6 copy-start.17
  120.2 5.6 copy-start.20
  123.1 2.3 copy-start.2
  123.1 2.7 copy-start.1
  123.5 4.8 copy-start.21
  123.5 5.3 copy-start.6
  125.3 3.3 copy-start.10
  128.2 5.9 %copy-start.12 = (f32[128,2,4]{0,2,1:T(4,128)S(1)}, f32[128,2,4]{0,2,1:T(4,128)}, u32[]{:S(2)}) copy-start(f32[128,2,4]{0,2,1:T(4,128)} %copy-done.11) | copy-start | bytes 12292
  128.2 5.9 %copy-start.14 = (f32[128,2,4]{0,2,1:T(4,128)S(1)}, f32[128,2,4]{0,2,1:T(4,128)}, u32[]{:S(2)}) copy-start(f32[128,2,4]{0,2,1:T(4,128)} %copy-done.13) | copy-start | bytes 12292
  128.2 5.9 %copy-start.16 = (f32[128,2,4]{0,2,1:T(4,128)S(1)}, f32[128,2,4]{0,2,1:T(4,128)}, u32[]{:S(2)}) copy-start(f32[128,2,4]{0,2,1:T(4,128)} %copy-done.15) | copy-start | bytes 12292
  128.2 5.9 %copy-start.18 = (f32[128,2,4]{0,2,1:T(4,128)S(1)}, f32[128,2,4]{0,2,1:T(4,128)}, u32[]{:S(2)}) copy-start(f32[128,2,4]{0,2,1:T(4,128)} %copy-done.17) | copy-start | bytes 12292
  128.2 138.3 %copy-start.7 = (bf16[128,256]{1,0:T(8,128)(2,1)S(1)}, bf16[128,256]{1,0:T(8,128)(2,1)}, u32[]{:S(2)}) copy-start(bf16[128,256]{1,0:T(8,128)(2,1)} %param.20) | copy-start | bytes 196612
  128.2 245.2 %all-gather.8.cloned.1.call-start = ((), (), s32[]{:S(2)}) async-start(), calls=%async_computation.3 | async-start | bytes 25559040 | tf_op jit(solution)/shard_map/all_gather | solution.py:21
  129.9 445.8 %reduce-scatter.2.cloned.1.call-start = ((), (), s32[]{:S(2)}) async-start(), calls=%async_computation.4 | async-start | bytes 1179648 | tf_op jit(solution)/shard_map/reduce_scatter | solution.py:155
  130.7 3.1 copy-start.3
  273.5 24.1 %copy-start.5 = (bf16[128,2048]{1,0:T(8,128)(2,1)S(1)}, bf16[128,2048]{1,0:T(8,128)(2,1)}, u32[]{:S(2)}) copy-start(bf16[128,2048]{1,0:T(8,128)(2,1)} %param.22) | copy-start | bytes 1572868
  297.6 190.4 %copy-start.19 = (f32[128,6]{0,1:T(8,128)S(1)}, f32[128,6]{0,1:T(8,128)}, u32[]{:S(2)}) copy-start(f32[128,6]{0,1:T(8,128)} %copy.92) | copy-start | bytes 9220
  297.9 190.1 %copy-start.8 = (bf16[128,256]{1,0:T(8,128)(2,1)S(1)}, bf16[128,256]{1,0:T(8,128)(2,1)}, u32[]{:S(2)}) copy-start(bf16[128,256]{1,0:T(8,128)(2,1)} %param.20) | copy-start | bytes 196612
  297.9 190.1 %copy-start.9 = (f32[128,6,64]{0,2,1:T(8,128)S(1)}, f32[128,6,64]{0,2,1:T(8,128)}, u32[]{:S(2)}) copy-start(f32[128,6,64]{0,2,1:T(8,128)} %convolution_bitcast_fusion.5) | copy-start | bytes 589828
Sparse Core Ops, SparseCore 0:
  128.3 88.1 all-gather.5
  218.7 154.6 all-gather.7
  491.0 84.6 reduce-scatter.1
